TPU v7x, 512 devices: a whole 4x4x16 slice. The times are simulated.
512 devices in a mesh: dp: 128 (over x_lo, y, z), mp: 4 (over x_hi, core).
Axes of the slice: x: 4 (x_hi: 2, x_lo: 2; x = x_hi * 2 + x_lo), y: 4, z: 16, core: 2. Of those that a mesh axis runs over, the one named last changes fastest.
Arguments:
- image: bfloat16 [98304, 1024], P('dp', 'mp'), may hold values from -0.59765625 to 0.59765625
- text: bfloat16 [98304, 1024], P('dp', 'mp'), may hold values from -0.59765625 to 0.59765625
Outputs:
- image_grad: float32 [98304, 1024], P(('dp', 'mp'))
- text_grad: float32 [98304, 1024], P(('dp', 'mp'))
- row_loss: float32 [98304], P(('dp', 'mp'))
All inputs are finite; a program needn't handle non-finite values.
Results may differ from a plain program's by a relative error of at most 0.0017.
Values may be sent and summed in bfloat16 or wider, within the bound.
A program may use at most 64 MiB of HBM per device.

v0:
```python
import jax
import jax.numpy as jnp
from jax import lax
from jax.sharding import PartitionSpec as P

TILES = 3


LOGIT_SCALE = 10.0
LOGIT_BIAS = -2.0


def shifted(block, axis, distance):
    devices = range(lax.axis_size(axis))
    route = [((i - distance) % len(devices), i) for i in devices]
    return lax.ppermute(block, axis, route)


def local(image, text):
    group_index = lax.axis_index("mp")
    my_rows = lax.all_to_all(image, "mp", split_axis=0, concat_axis=1, tiled=True)
    quarter = my_rows.shape[0]
    block_rows = image.shape[0]
    row_ids = lax.broadcasted_iota(jnp.int32, (quarter, block_rows), 0) + group_index * quarter
    col_ids = lax.broadcasted_iota(jnp.int32, (quarter, block_rows), 1)
    own_positive = (row_ids == col_ids).astype(jnp.float32)
    zero_positive = jnp.zeros((quarter, block_rows), jnp.float32)
    image_accum = jnp.zeros(my_rows.shape, jnp.float32)
    row_total = jnp.zeros((quarter,), jnp.float32)
    text_cols = text
    carried = None
    for s in range(TILES):
        if s > 0:
            text_cols = shifted(text_cols, "dp", 1)
        text_full = lax.all_gather(text_cols, "mp", axis=1, tiled=True)
        logit_tile = (
            LOGIT_SCALE
            * lax.dot_general(
                my_rows, text_full, (((1,), (1,)), ((), ())), preferred_element_type=jnp.float32
            )
            + LOGIT_BIAS
        )
        positive = own_positive if s == 0 else zero_positive
        label_sign = 2.0 * positive - 1.0
        row_total = row_total + jnp.sum(jax.nn.softplus(-label_sign * logit_tile), axis=1)
        coefficient = (jax.nn.sigmoid(logit_tile) - positive).astype(jnp.bfloat16)
        image_accum = image_accum + LOGIT_SCALE * jnp.dot(
            coefficient, text_full, preferred_element_type=jnp.float32
        )
        contribution = LOGIT_SCALE * lax.dot_general(
            coefficient, my_rows, (((0,), (0,)), ((), ())), preferred_element_type=jnp.float32
        )
        if s == 0:
            carried = contribution
        else:
            carried = shifted(carried, "dp", 1) + contribution
    home_grad = shifted(carried, "dp", -(TILES - 1))
    text_result = lax.psum_scatter(home_grad, "mp", scatter_dimension=0, tiled=True)
    return (image_accum, text_result, row_total)


def solution(mesh):
    in_specs = (P("dp", "mp"), P("dp", "mp"))
    out_specs = (P(("dp", "mp"), None), P(("dp", "mp"), None), P(("dp", "mp")))
    return jax.shard_map(local, mesh=mesh, in_specs=in_specs, out_specs=out_specs, check_vma=False)
```

profile of v0, /device:TPU:1, one launch (start us, length us, event | category | flops | bytes accessed | tf_op | source)
XLA Modules:
  0.0 451.6 jit_solution(16354524757578665672)
XLA Ops:
  7.9 10.3 %all-to-all-start = ((bf16[4,192,256]{2,1,0:T(8,128)(2,1)}), bf16[4,192,256]{2,1,0:T(8,128)(2,1)S(1)}, u32[]{:S(2)}, u32[]{:S(2)}) async-start(bf16[4,192,256]{2,1,0:T(8,128)(2,1)} %bitcast.23), calls=%async_computation | async-start | bytes 786432 | tf_op jit(solution)/shard_map/all_to_all | solution.py:21
  18.2 8.1 %all-to-all-done = bf16[4,192,256]{2,1,0:T(8,128)(2,1)S(1)} async-done(((bf16[4,192,256]{2,1,0:T(8,128)(2,1)}), bf16[4,192,256]{2,1,0:T(8,128)(2,1)S(1)}, u32[]{:S(2)}, u32[]{:S(2)}) %all-to-all-start) | async-done | bytes 393248 | tf_op jit(solution)/shard_map/all_to_all | solution.py:21
  26.3 21.1 %all-gather.4.cloned.1.call-done = bf16[768,1024]{1,0:T(8,128)(2,1)} async-done(((bf16[768,256]{1,0:T(8,128)(2,1)}), bf16[768,1024]{1,0:T(8,128)(2,1)}) %all-gather.4.cloned.1.call-update) | async-done | bytes 1572880 | tf_op jit(solution)/shard_map/all_gather | solution.py:35
  47.4 2.4 fusion.4
  49.9 0.8 copy-done.8
  50.7 2.3 convolution_multiply_fusion
  53.0 3.2 collective-permute-start.2
  56.2 3.2 collective-permute-start
  59.4 78.5 %collective-permute-done = bf16[768,256]{1,0:T(8,128)(2,1)} collective-permute-done((bf16[768,256]{1,0:T(8,128)(2,1)S(1)}, bf16[768,256]{1,0:T(8,128)(2,1)}, u32[]{:S(2)}, u32[]{:S(2)}) %collective-permute-start) | collective-permute-done | bytes 393248 | tf_op jit(solution)/shard_map/ppermute | solution.py:16
  137.9 1.9 collective-permute-start.1
  139.9 26.5 %all-gather.6.cloned.1.call-done = bf16[768,1024]{1,0:T(8,128)(2,1)} async-done(((bf16[768,256]{1,0:T(8,128)(2,1)}), bf16[768,1024]{1,0:T(8,128)(2,1)}) %all-gather.6.cloned.1.call-update) | async-done | bytes 1572880 | tf_op jit(solution)/shard_map/all_gather | solution.py:35
  166.3 2.4 fusion.5
  168.8 2.3 multiply_add_fusion.1
  171.0 3.2 collective-permute-start.3
  174.3 30.6 %all-gather.8.cloned.1.call-done = bf16[768,1024]{1,0:T(8,128)(2,1)} async-done(((bf16[768,256]{1,0:T(8,128)(2,1)}), bf16[768,1024]{1,0:T(8,128)(2,1)}) %all-gather.8.cloned.1.call-update) | async-done | bytes 1572880 | tf_op jit(solution)/shard_map/all_gather | solution.py:35
  204.9 2.4 fusion.6
  208.2 39.3 %collective-permute-done.3 = f32[768,1024]{1,0:T(8,128)S(1)} collective-permute-done((f32[768,1024]{1,0:T(8,128)}, f32[768,1024]{1,0:T(8,128)S(1)}, u32[]{:S(2)}, u32[]{:S(2)}) %collective-permute-start.3) | collective-permute-done | bytes 3145760 | tf_op jit(solution)/shard_map/ppermute | solution.py:16
  247.4 0.7 multiply_add_fusion
  248.1 3.8 collective-permute-start.4
  252.0 133.2 %collective-permute-done.4 = f32[768,1024]{1,0:T(8,128)S(1)} collective-permute-done((f32[768,1024]{1,0:T(8,128)S(1)}, f32[768,1024]{1,0:T(8,128)S(1)}, u32[]{:S(2)}, u32[]{:S(2)}) %collective-permute-start.4) | collective-permute-done | bytes 3145760 | tf_op jit(solution)/shard_map/ppermute | solution.py:16
  385.2 1.6 copy-done
  386.9 2.3 fusion.8
  390.8 1.4 fusion
  392.2 52.9 %reduce-scatter.2.cloned.1.call-done = f32[192,1024]{1,0:T(8,128)} async-done(((f32[768,1024]{1,0:T(8,128)}), f32[192,1024]{1,0:T(8,128)}) %reduce-scatter.2.cloned.1.call-update) | async-done | bytes 786448 | tf_op jit(solution)/shard_map/reduce_scatter | solution.py:58
  (31 shorter events, 3.4 us)
Async XLA Ops:
  7.2 40.2 %all-gather.4.cloned.1.call-start = ((), (), s32[]{:S(2)}) async-start(), calls=%async_computation.2 | async-start | bytes 1966080 | tf_op jit(solution)/shard_map/all_gather | solution.py:35
  7.9 18.4 %all-to-all-start = ((bf16[4,192,256]{2,1,0:T(8,128)(2,1)}), bf16[4,192,256]{2,1,0:T(8,128)(2,1)S(1)}, u32[]{:S(2)}, u32[]{:S(2)}) async-start(bf16[4,192,256]{2,1,0:T(8,128)(2,1)} %bitcast.23), calls=%async_computation | async-start | bytes 786432 | tf_op jit(solution)/shard_map/all_to_all | solution.py:21
  18.2 148.1 %all-gather.6.cloned.1.call-start = ((), (), s32[]{:S(2)}) async-start(), calls=%async_computation.3 | async-start | bytes 1966080 | tf_op jit(solution)/shard_map/all_gather | solution.py:35
  49.8 0.8 copy-start.8
  49.9 6.3 %copy-start.5 = (bf16[768,256]{1,0:T(8,128)(2,1)S(1)}, bf16[768,256]{1,0:T(8,128)(2,1)}, u32[]{:S(2)}) copy-start(bf16[768,256]{1,0:T(8,128)(2,1)} %param.3) | copy-start | bytes 1179652
  53.0 115.8 %collective-permute-start.2 = (f32[768,1024]{1,0:T(8,128)}, f32[768,1024]{1,0:T(8,128)S(1)}, u32[]{:S(2)}, u32[]{:S(2)}) collective-permute-start(f32[768,1024]{1,0:T(8,128)} %convolution_multiply_fusion), channel_id=1, source_target_pairs={{508,0},{0,4},{4,8},{8,12},{12,16},{16,20},{20,24},{24,28},{28,32}... | collective-permute-start | bytes 9437192 | tf_op jit(solution)/shard_map/ppermute | solution.py:16
  56.2 81.7 %collective-permute-start = (bf16[768,256]{1,0:T(8,128)(2,1)S(1)}, bf16[768,256]{1,0:T(8,128)(2,1)}, u32[]{:S(2)}, u32[]{:S(2)}) collective-permute-start(bf16[768,256]{1,0:T(8,128)(2,1)S(1)} %copy-done.5), channel_id=1, source_target_pairs={{508,0},{0,4},{4,8},{8,12},{12,16},{16,20},{20,24},{24,28},{28,32}... | collective-permute-start | bytes 1179656 | tf_op jit(solution)/shard_map/ppermute | solution.py:16
  137.9 67.0 %all-gather.8.cloned.1.call-start = ((), (), s32[]{:S(2)}) async-start(), calls=%async_computation.4 | async-start | bytes 1966080 | tf_op jit(solution)/shard_map/all_gather | solution.py:35
  137.9 36.3 %collective-permute-start.1 = (bf16[768,256]{1,0:T(8,128)(2,1)}, bf16[768,256]{1,0:T(8,128)(2,1)}, u32[]{:S(2)}, u32[]{:S(2)}) collective-permute-start(bf16[768,256]{1,0:T(8,128)(2,1)} %collective-permute-done), channel_id=1, source_target_pairs={{508,0},{0,4},{4,8},{8,12},{12,16},{16,20},{20,24},{24,28},{28,32}... | collective-permute-start | bytes 1179656 | tf_op jit(solution)/shard_map/ppermute | solution.py:16
  168.7 2.3 copy-start.1
  171.0 76.4 %collective-permute-start.3 = (f32[768,1024]{1,0:T(8,128)}, f32[768,1024]{1,0:T(8,128)S(1)}, u32[]{:S(2)}, u32[]{:S(2)}) collective-permute-start(f32[768,1024]{1,0:T(8,128)} %multiply_add_fusion.1), channel_id=1, source_target_pairs={{508,0},{0,4},{4,8},{8,12},{12,16},{16,20},{20,24},{24,28},{28,32}... | collective-permute-start | bytes 9437192 | tf_op jit(solution)/shard_map/ppermute | solution.py:16
  174.3 270.8 %reduce-scatter.2.cloned.1.call-start = ((), (), s32[]{:S(2)}) async-start(), calls=%async_computation.5 | async-start | bytes 3932160 | tf_op jit(solution)/shard_map/reduce_scatter | solution.py:58
  207.3 0.9 copy-start.3
  248.1 137.1 %collective-permute-start.4 = (f32[768,1024]{1,0:T(8,128)S(1)}, f32[768,1024]{1,0:T(8,128)S(1)}, u32[]{:S(2)}, u32[]{:S(2)}) collective-permute-start(f32[768,1024]{1,0:T(8,128)S(1)} %multiply_add_fusion), channel_id=1, source_target_pairs={{8,0},{12,4},{16,8},{20,12},{24,16},{28,20},{32,24},{36,28},{40,32... | collective-permute-start | bytes 9437192 | tf_op jit(solution)/shard_map/ppermute | solution.py:16
  385.2 1.6 copy-start
  386.9 2.3 copy-start.2
  386.9 2.3 copy-start.6
  389.2 1.1 copy-start.4
  389.2 1.6 copy-start.7
Sparse Core Ops, SparseCore 0:
  10.1 37.2 all-gather.3
  138.0 28.2 all-gather.5
  174.4 30.4 all-gather.7
  387.0 58.0 reduce-scatter.1
where the time goes:
time: 452 us
  waiting for transfers between devices  391 us (87%)
  starting transfers between devices  25.7 us (6%)
  matrix products  16.7 us (4%)
  between operations  13.9 us (3%)
    ppermute x5, waiting for transfers between devices, shifted(): return lax.ppermute(block, axis, route)  251 us
    all_gather x3, waiting for transfers between devices, local(): text_full = lax.all_gather(text_cols, 'mp', axis=1, tiled=True)  78.1 us
    reduce_scatter x1, waiting for transfers between devices, local(): lax.psum_scatter(home_grad, 'mp', scatter_dimension=0, tiled=True)  52.9 us
    ppermute x5, starting transfers between devices, shifted(): return lax.ppermute(block, axis, route)  15.3 us
    all_to_all x1, starting transfers between devices, local(): lax.all_to_all(image, 'mp', split_axis=0, concat_axis=1, tiled=True)  10.3 us
  transfers between devices with their start and end apart: 10, of which 8 were waited for; matrix products, arithmetic and copies ran while one was open for 3% of the time, Pallas kernels for 0%

commit v1 on v0

v1 whole, which is shorter than its diff:
```python
import jax
import jax.numpy as jnp
from jax import lax
from jax.sharding import PartitionSpec as P
import jax.experimental.pallas as pl
import jax.experimental.pallas.tpu as pltpu

TILES = 3
LOGIT_SCALE = 10.0
LOGIT_BIAS = -2.0
MESH = pl.DeviceIdType.MESH

GROUPS = 128
HALF = GROUPS // 2
PARTS = 4
CHUNK = 192
COLS = 256
SLOTS = TILES * PARTS


def kernel(img, txt, gi, gt, loss, xb, yb, lacc, send, recv, local):
    g, m = lax.axis_index("dp"), lax.axis_index("mp")
    sib = m + 1 - 2 * (m % 2)
    par = (m + 2) % PARTS
    base = 2 * (m // 2)
    up, down = (g + 1) % GROUPS, (g + GROUPS - 1) % GROUPS
    flows = ((img, xb, down, g % HALF == 0), (txt, yb, up, g % HALF == HALF - 1))

    def put(t, src, q, kind, slot, device, whole=False):
        dst = flows[t][1].at[q, pl.ds(slot, PARTS)] if whole else flows[t][1].at[q, slot]
        return pltpu.make_async_remote_copy(
            src_ref=src,
            dst_ref=dst,
            send_sem=send.at[t, kind, slot],
            recv_sem=recv.at[t, kind, slot],
            device_id=device,
            device_id_type=MESH,
        )

    def arrived(t, kind, slot, whole=False):
        src = flows[t][1].at[0, pl.ds(0, PARTS)] if whole else flows[t][1].at[0, 0]
        put(t, src, 0, kind, 0 if whole else slot, (g, sib), whole).wait_recv()

    own = [pltpu.make_async_copy(flows[t][0], flows[t][1].at[m, pl.ds(0, PARTS)], local.at[t]) for t in range(2)]
    for c in own:
        c.start()

    barrier = pltpu.get_barrier_semaphore()
    for device in ((g, sib), (g, par), (up, m), (down, m), (up, par), (down, par)):
        pl.semaphore_signal(barrier, inc=1, device_id=device, device_id_type=MESH)
    pl.semaphore_wait(barrier, 6)

    for k in range(PARTS):
        c = (base + 2 + k) % PARTS
        for t in range(2):
            entry, _, nxt, _ = flows[t]
            put(t, entry.at[k], m, 0, PARTS + k, (nxt, m)).start()
            put(t, entry.at[c], m, 2, c, (g, par)).start()
        if k == 0:
            for t in range(2):
                put(t, flows[t][0], m, 1, 0, (g, sib), True).start()
    gi[...] = jnp.zeros_like(gi)
    gt[...] = jnp.zeros_like(gt)
    lacc[...] = jnp.zeros_like(lacc)
    for c in own:
        c.wait()

    def slot_of(i):
        return PARTS * (i // PARTS) + (base + i) % PARTS

    def own_quarters(i):
        for e in range(2):
            o = PARTS + 2 * i + e
            for t in range(2):
                _, buf, nxt, _ = flows[t]
                arrived(t, 0, o)

                @pl.when(o < 2 * PARTS)
                def _():
                    put(t, buf.at[m, o], m, 0, o + PARTS, (nxt, m)).start()

                put(t, buf.at[m, o], m, 1, o, (g, sib)).start()

    def partner_quarters(i):
        slot = slot_of(i)
        for t in range(2):
            _, buf, nxt, across = flows[t]
            arrived(t, 2, slot)

            @pl.when(i < 2 * PARTS)
            def _():
                q = jnp.where(across, m, par)
                to = jnp.where(across, par, m)
                there = PARTS * (i // PARTS) + (2 * (to // 2) + i) % PARTS
                put(t, buf.at[q, there], q, 2, there + PARTS, (nxt, to)).start()

            put(t, buf.at[par, slot], par, 3, slot, (g, sib)).start()

    def tile(t, slot):
        mine, other, out = (xb, yb, gi) if t == 1 else (yb, xb, gt)
        acc = None
        for q in range(PARTS):
            d = lax.dot_general(
                mine[q, m], other[q, slot], (((1,), (1,)), ((), ())), preferred_element_type=jnp.float32
            )
            acc = d if acc is None else acc + d
        logit = LOGIT_SCALE * acc + LOGIT_BIAS
        rows = lax.broadcasted_iota(jnp.int32, (CHUNK, CHUNK), 0)
        cols = lax.broadcasted_iota(jnp.int32, (CHUNK, CHUNK), 1)
        positive = (rows - cols) == jnp.where(slot == m, 0, 4 * CHUNK)
        if t == 1:
            x = jnp.where(positive, -logit, logit)
            lacc[...] += jnp.maximum(x, 0.0) + jnp.log1p(jnp.exp(-jnp.abs(x)))
        coefficient = 1.0 / (1.0 + jnp.exp(-logit)) - jnp.where(positive, 1.0, 0.0)
        coefficient = coefficient.astype(jnp.bfloat16)
        for q in range(PARTS):
            out[:, pl.ds(q * COLS, COLS)] += jnp.dot(coefficient, other[q, slot], preferred_element_type=jnp.float32)

    def tiles(i):
        slot = slot_of(i)
        for t in (1, 0):
            tile(t, slot)

    def from_core(i):
        slot = slot_of(i)
        for t in range(2):
            arrived(t, 3, slot)

            @pl.when(i >= PARTS)
            def _():
                arrived(t, 1, slot)

    own_quarters(0)
    partner_quarters(0)
    own_quarters(1)
    partner_quarters(1)
    for t in range(2):
        arrived(t, 1, 0, True)
    from_core(0)
    from_core(1)

    @pl.loop(1, SLOTS + 1)
    def _(i):
        @pl.when((i >= 2) & (i < 4))
        def _():
            own_quarters(i)

        @pl.when((i >= 2) & (i < SLOTS))
        def _():
            partner_quarters(i)

        @pl.when(i >= 3)
        def _():
            from_core(i - 1)

        tiles(i - 1)

    gi[...] *= LOGIT_SCALE
    gt[...] *= LOGIT_SCALE
    loss[...] = jnp.sum(jnp.transpose(lacc[...]), axis=0, keepdims=True)

    for t in range(2):
        put(t, flows[t][0], m, 1, 0, (g, sib), True).wait_send()

        @pl.loop(0, SLOTS)
        def _(slot):
            for kind in range(PARTS):
                def done():
                    put(t, flows[t][1].at[0, 0], 0, kind, slot, (g, sib)).wait_send()

                if kind < 2:
                    pl.when(slot >= PARTS)(done)
                else:
                    done()


def local(image, text):
    rows, cols = image.shape
    width = cols * PARTS
    block = (PARTS, rows // PARTS, cols)
    flops = 2 * 4 * TILES * CHUNK * rows * width
    gi, gt, loss = pl.pallas_call(
        kernel,
        out_shape=(
            jax.ShapeDtypeStruct((CHUNK, width), jnp.float32),
            jax.ShapeDtypeStruct((CHUNK, width), jnp.float32),
            jax.ShapeDtypeStruct((1, CHUNK), jnp.float32),
        ),
        in_specs=[pl.BlockSpec(memory_space=pl.ANY)] * 2,
        out_specs=[pl.BlockSpec(memory_space=pltpu.VMEM)] * 3,
        scratch_shapes=[
            pltpu.VMEM((PARTS, SLOTS, CHUNK, COLS), jnp.bfloat16),
            pltpu.VMEM((PARTS, SLOTS, CHUNK, COLS), jnp.bfloat16),
            pltpu.VMEM((CHUNK, CHUNK), jnp.float32),
            pltpu.SemaphoreType.DMA((2, PARTS, SLOTS)),
            pltpu.SemaphoreType.DMA((2, PARTS, SLOTS)),
            pltpu.SemaphoreType.DMA((2,)),
        ],
        compiler_params=pltpu.CompilerParams(
            collective_id=0, has_side_effects=True, vmem_limit_bytes=40 * 1024 * 1024
        ),
        cost_estimate=pl.CostEstimate(
            flops=flops, bytes_accessed=4 * rows * cols * 2, transcendentals=4 * TILES * CHUNK * rows
        ),
    )(image.reshape(block), text.reshape(block))
    return gi, gt, loss.reshape(CHUNK)


def solution(mesh):
    in_specs = (P("dp", "mp"), P("dp", "mp"))
    out_specs = (P(("dp", "mp"), None), P(("dp", "mp"), None), P(("dp", "mp")))
    return jax.shard_map(local, mesh=mesh, in_specs=in_specs, out_specs=out_specs, check_vma=False)
```

time: 452 us -> 82.8 us (0.18)
  the two profiles are of different devices: /device:TPU:1 before, /device:TPU:57 now
where the time goes in v1:
time: 82.8 us; the launch traced here: 82.6 us
  Pallas kernels  77.6 us (94%)
  local copies, waits for them, and re-layouts  4.31 us (5%)
    pallas_call x1, Pallas kernels, local(): pl.pallas_call(kernel, out_shape=(jax.ShapeDtypeStruct((CHUNK, width), jn...  77.6 us
    unnamed x7, local copies, waits for them, and re-layouts  4.31 us

profile of v1, /device:TPU:57, one launch (start us, length us, event | category | flops | bytes accessed | tf_op | source)
XLA Modules:
  0.0 82.6 jit_solution(6225834059425403761)
XLA Ops:
  0.6 0.0 copy-start
  0.6 1.0 %copy-done = bf16[768,256]{1,0:T(8,128)(2,1)S(1)} copy-done((bf16[768,256]{1,0:T(8,128)(2,1)S(1)}, bf16[768,256]{1,0:T(8,128)(2,1)}, u32[]{:S(2)}) %copy-start) | copy-done | bytes 393240
  1.6 0.0 copy-start.1
  1.6 1.0 %copy-done.1 = bf16[768,256]{1,0:T(8,128)(2,1)S(1)} copy-done((bf16[768,256]{1,0:T(8,128)(2,1)S(1)}, bf16[768,256]{1,0:T(8,128)(2,1)}, u32[]{:S(2)}) %copy-start.1) | copy-done | bytes 393240
  2.6 77.6 %shard_map.49 = (f32[192,1024]{1,0:T(8,128)S(1)}, f32[192,1024]{1,0:T(8,128)S(1)}, f32[1,192]{1,0:T(1,128)S(1)}) custom-call(bf16[4,192,256]{2,1,0:T(8,128)(2,1)S(1)} %bitcast.4, bf16[4,192,256]{2,1,0:T(8,128)(2,1)S(1)} %bitcast.5), custom_call_target="tpu_custom_call" | custom-call | flops 3623878656 | bytes 1572864 | tf_op jit(solution)/shard_map/pallas_call | solution.py:182
  80.3 0.9 %copy.8 = f32[192,1024]{1,0:T(8,128)} copy(f32[192,1024]{1,0:T(8,128)S(1)} %get-tuple-element.12) | data formatting | bytes 1572864
  81.1 0.9 %copy.9 = f32[192,1024]{1,0:T(8,128)} copy(f32[192,1024]{1,0:T(8,128)S(1)} %get-tuple-element.13) | data formatting | bytes 1572864
  82.0 0.6 copy.10
Async XLA Ops:
  0.6 1.0 %copy-start = (bf16[768,256]{1,0:T(8,128)(2,1)S(1)}, bf16[768,256]{1,0:T(8,128)(2,1)}, u32[]{:S(2)}) copy-start(bf16[768,256]{1,0:T(8,128)(2,1)} %param.2) | copy-start | bytes 1179652
  1.6 1.0 %copy-start.1 = (bf16[768,256]{1,0:T(8,128)(2,1)S(1)}, bf16[768,256]{1,0:T(8,128)(2,1)}, u32[]{:S(2)}) copy-start(bf16[768,256]{1,0:T(8,128)(2,1)} %param.3) | copy-start | bytes 1179652

commit v2 on v1

v2 whole, which is shorter than its diff:
```python
import jax
import jax.numpy as jnp
from jax import lax
from jax.sharding import PartitionSpec as P
import jax.experimental.pallas as pl
import jax.experimental.pallas.tpu as pltpu

TILES = 3
LOGIT_SCALE = 10.0
LOGIT_BIAS = -2.0
MESH = pl.DeviceIdType.MESH

GROUPS = 128
HALF = GROUPS // 2
PARTS = 4
CHUNK = 192
COLS = 256
X_AHEAD = 2
GATES = (8, 7)
LATE = 9
SHIFT = 4
ALONG = 16
STEPS = 21
SLOTS = TILES * PARTS


def kernel(img, txt, gi, gt, loss, held, grads, lacc, send, recv, local):
    g, m = lax.axis_index("dp"), lax.axis_index("mp")
    sib = m + 1 - 2 * (m % 2)
    par = (m + 2) % PARTS
    base = 2 * (m // 2)
    up, down = (g + 1) % GROUPS, (g + GROUPS - 1) % GROUPS
    z = g % ALONG
    flows = (
        (img, held.at[0], down, g % HALF == 0, g % HALF == HALF - 1, g % HALF == HALF - 2),
        (txt, held.at[1], up, g % HALF == HALF - 1, g % HALF == 0, g % HALF == 1),
    )

    def put(t, src, q, kind, slot, device, whole=False, sem=None):
        dst = flows[t][1].at[q, pl.ds(slot, PARTS)] if whole else flows[t][1].at[q, slot]
        return pltpu.make_async_remote_copy(
            src_ref=src,
            dst_ref=dst,
            send_sem=send.at[t, kind if sem is None else sem, slot],
            recv_sem=recv.at[t, kind, slot],
            device_id=device,
            device_id_type=MESH,
        )

    def arrived(t, kind, slot, whole=False):
        ref = held.at[t, 0, pl.ds(0, PARTS)] if whole else held.at[t, 0, 0]
        pltpu.make_async_remote_copy(
            src_ref=ref,
            dst_ref=ref,
            send_sem=send.at[t, kind, slot],
            recv_sem=recv.at[t, kind, slot],
            device_id=(g, sib),
            device_id_type=MESH,
        ).wait_recv()

    own = [pltpu.make_async_copy(flows[t][0], flows[t][1].at[m, pl.ds(0, PARTS)], local.at[t]) for t in range(2)]
    for c in own:
        c.start()

    barrier = pltpu.get_barrier_semaphore()
    for device in ((g, sib), (g, par), (up, m), (down, m), (up, par), (down, par)):
        pl.semaphore_signal(barrier, inc=1, device_id=device, device_id_type=MESH)
    pl.semaphore_wait(barrier, 6)

    def onward(t, kind, slot):
        _, buf, nxt, *_ = flows[t]
        q = jnp.where(kind == 0, m, par)
        put(t, buf.at[q, slot - PARTS], q, kind, slot, (nxt, m)).start()

    def to_partner(j):
        c = (base + 2 + j) % PARTS
        for t in range(2):
            put(t, flows[t][0].at[c], m, 2, c, (g, par)).start()

    for k in range(PARTS):
        for t in range(2):
            entry, _, nxt, across, *_ = flows[t]
            pl.when(jnp.logical_not(across))(put(t, entry.at[k], m, 0, PARTS + k, (nxt, m)).start)
        if k < X_AHEAD:
            to_partner(k)
        if k == 0:
            for t in range(2):
                put(t, flows[t][0], m, 1, 0, (g, sib), True).start()
    grads[...] = jnp.zeros_like(grads)
    lacc[...] = jnp.zeros_like(lacc)
    for c in own:
        c.wait()

    def chunk_of(t, i):
        _, _, _, _, late, second = flows[t]
        absolute = ((i >= PARTS) & late) | ((i >= 2 * PARTS) & second)
        return PARTS * (i // PARTS) + (jnp.where(absolute, 0, base) + i) % PARTS

    def over_x(j):
        pl.when(j < PARTS - X_AHEAD)(lambda: to_partner(j + X_AHEAD))
        c = (base + j) % PARTS
        for t in range(2):
            _, buf, _, across, _, _ = flows[t]
            arrived(t, 2, c)
            pl.when(jnp.logical_not(across))(lambda: onward(t, 2, c + PARTS))
            put(t, buf.at[par, c], par, 3, c, (g, sib)).start()

    def shifts(t):
        if t == 0:
            return 0, 0
        return jnp.where(z == 0, SHIFT, 0), jnp.where(z <= 1, SHIFT, 0)

    def arrivals(n, t):
        _, buf, nxt, across, late, second = flows[t]
        normal = jnp.logical_not(late | second)
        n1, n2 = n - shifts(t)[0], n - shifts(t)[1]
        slot = jnp.where((n1 >= 0) & (n1 < 4) & jnp.logical_not(late), 4 + n1, -1)
        slot = jnp.where(normal & (n2 >= 5) & (n2 < 12) & (n2 % 2 == 1), 8 + (n2 - 5) // 2, slot)
        slot = jnp.where(second & (n >= LATE + 2) & (n < LATE + 6), n - LATE + 6, slot)
        slot = jnp.where(late & (n >= LATE) & (n < LATE + 8), n - LATE + 4, slot)

        @pl.when(slot >= 0)
        def _():
            arrived(t, 0, slot)

            @pl.when(late)
            def _():
                put(t, buf.at[m, slot], m, 2, slot, (g, par), sem=PARTS).start()
                pl.when(slot < 2 * PARTS)(lambda: onward(t, 0, slot + PARTS))

            put(t, buf.at[m, slot], m, 1, slot, (g, sib)).start()

        i = jnp.where(jnp.logical_not(late) & (n1 >= 4) & (n1 < 12) & (n1 % 2 == 0), 4 + (n1 - 4) // 2, -1)
        i = jnp.where(normal & (n2 >= 12) & (n2 < 16), n2 - 4, i)
        i = jnp.where(second & (n >= LATE + 4) & (n < LATE + 8), n - LATE + 4, i)
        i = jnp.where(late & (n >= LATE + 2) & (n < LATE + 10), n - LATE + 2, i)

        @pl.when(i >= 0)
        def _():
            half = chunk_of(t, i)
            arrived(t, 2, half)
            pl.when(late & (half < 2 * PARTS))(lambda: onward(t, 2, half + PARTS))
            put(t, buf.at[par, half], par, 3, half, (g, sib)).start()

    def sends(n, t):
        _, _, _, across, late, _ = flows[t]
        normal = jnp.logical_not(across | late)
        n1 = n - shifts(t)[0]

        @pl.when(normal & (n1 >= 0) & (n1 < 8) & (n1 % 2 == 1))
        def _():
            onward(t, 0, 2 * PARTS + n1 // 2)

        @pl.when(normal & (n1 >= 8) & (n1 < 12))
        def _():
            onward(t, 2, chunk_of(t, n1 - 4) + PARTS)

        gate = GATES[t]

        @pl.when(across & (n >= gate) & (n <= gate + 5))
        def _():
            @pl.when(n == gate)
            def _():
                for k in range(3):
                    onward(t, 0, PARTS + k)

            pl.when(n > gate)(lambda: onward(t, 0, n - gate + 2 + PARTS))

    def tile(t, slot):
        def rows_of(q):
            return held[t, q, pl.ds(slot, 2)].reshape(2 * CHUNK, COLS)

        acc = None
        for q in range(PARTS):
            d = lax.dot_general(
                held[1 - t, q, m], rows_of(q), (((1,), (1,)), ((), ())), preferred_element_type=jnp.float32
            )
            acc = d if acc is None else acc + d
        logit = LOGIT_SCALE * acc + LOGIT_BIAS
        rows = lax.broadcasted_iota(jnp.int32, acc.shape, 0)
        cols = lax.broadcasted_iota(jnp.int32, acc.shape, 1)
        positive = (cols - rows) == jnp.where(slot < PARTS, (m - slot) * CHUNK, 4 * CHUNK)
        @pl.when(t == 1)
        def _():
            x = jnp.where(positive, -logit, logit)
            lacc[...] += jnp.maximum(x, 0.0) + jnp.log1p(jnp.exp(-jnp.abs(x)))
        coefficient = 1.0 / (1.0 + jnp.exp(-logit)) - jnp.where(positive, 1.0, 0.0)
        coefficient = coefficient.astype(jnp.bfloat16)
        for q in range(PARTS):
            grads[t, :, pl.ds(q * COLS, COLS)] += jnp.dot(coefficient, rows_of(q), preferred_element_type=jnp.float32)

    def reached(n, t):
        _, _, _, _, late, second = flows[t]
        n1, n2 = n - shifts(t)[0], n - shifts(t)[1]
        own_block = jnp.where(n < 8, jnp.clip(n - 3, 0, 3), PARTS)
        farther = jnp.where(second, n - LATE + 4, n2 - 4)
        chunks = jnp.maximum(jnp.maximum(own_block, jnp.minimum(n1 - 4, 2 * PARTS)), farther)
        chunks = jnp.where(late, jnp.maximum(own_block, n - LATE + 2), chunks)
        return jnp.minimum(chunks, SLOTS) // 2

    apart = flows[0][4] | flows[1][4] | flows[0][5] | flows[1][5] | (z <= 1)
    steps = jnp.where(apart, STEPS, STEPS - 4)

    @pl.loop(0, steps)
    def _(n):
        pl.when((n < 2 * PARTS) & (n % 2 == 1))(lambda: over_x(n // 2))
        for t in range(2):
            arrivals(n, t)
        for t in range(2):
            sends(n, t)

        @pl.when(n == 4)
        def _():
            for t in range(2):
                arrived(t, 1, 0, True)
                arrived(t, 3, base)
                arrived(t, 3, base + 1)

        def either(t, of):
            return jnp.where(t == 1, of(1), of(0))

        @pl.loop(0, 2)
        def _(k):
            t = 1 - k

            @pl.loop(either(t, lambda t: reached(n - 1, t)), either(t, lambda t: reached(n, t)))
            def _(i):
                slot = either(t, lambda t: chunk_of(t, 2 * i))
                for k in range(2):
                    pl.when(i >= PARTS // 2)(lambda: arrived(t, 1, slot + k))
                    pl.when(i >= 1)(lambda: arrived(t, 3, slot + k))
                tile(t, slot)

    gi[...] = grads[1] * LOGIT_SCALE
    gt[...] = grads[0] * LOGIT_SCALE
    loss[...] = jnp.sum(jnp.transpose(lacc[...]), axis=0, keepdims=True)

    for t in range(2):
        put(t, flows[t][0], m, 1, 0, (g, sib), True).wait_send()

        @pl.loop(0, SLOTS)
        def _(slot):
            def done(kind):
                put(t, flows[t][1].at[0, 0], 0, kind, slot, (g, sib)).wait_send()

            done(3)
            pl.when((slot < PARTS) | jnp.logical_not(flows[t][3]))(lambda: done(2))

            @pl.when(slot >= PARTS)
            def _():
                done(0)
                done(1)
                pl.when(flows[t][4])(lambda: done(PARTS))


def local(image, text):
    rows, cols = image.shape
    width = cols * PARTS
    block = (PARTS, rows // PARTS, cols)
    flops = 2 * 4 * TILES * CHUNK * rows * width
    gi, gt, loss = pl.pallas_call(
        kernel,
        out_shape=(
            jax.ShapeDtypeStruct((CHUNK, width), jnp.float32),
            jax.ShapeDtypeStruct((CHUNK, width), jnp.float32),
            jax.ShapeDtypeStruct((1, CHUNK), jnp.float32),
        ),
        in_specs=[pl.BlockSpec(memory_space=pl.ANY)] * 2,
        out_specs=[pl.BlockSpec(memory_space=pltpu.VMEM)] * 3,
        scratch_shapes=[
            pltpu.VMEM((2, PARTS, SLOTS, CHUNK, COLS), jnp.bfloat16),
            pltpu.VMEM((2, CHUNK, width), jnp.float32),
            pltpu.VMEM((CHUNK, 2 * CHUNK), jnp.float32),
            pltpu.SemaphoreType.DMA((2, PARTS + 1, SLOTS)),
            pltpu.SemaphoreType.DMA((2, PARTS, SLOTS)),
            pltpu.SemaphoreType.DMA((2,)),
        ],
        compiler_params=pltpu.CompilerParams(
            collective_id=0, has_side_effects=True, vmem_limit_bytes=40 * 1024 * 1024
        ),
        cost_estimate=pl.CostEstimate(
            flops=flops, bytes_accessed=4 * rows * cols * 2, transcendentals=4 * TILES * CHUNK * rows
        ),
    )(image.reshape(block), text.reshape(block))
    return gi, gt, loss.reshape(CHUNK)


def solution(mesh):
    in_specs = (P("dp", "mp"), P("dp", "mp"))
    out_specs = (P(("dp", "mp"), None), P(("dp", "mp"), None), P(("dp", "mp")))
    return jax.shard_map(local, mesh=mesh, in_specs=in_specs, out_specs=out_specs, check_vma=False)
```

time: 82.8 us -> 70.7 us (0.85)
  the two profiles are of different devices: /device:TPU:57 before, /device:TPU:1 now
where the time goes in v2:
time: 70.7 us; the launch traced here: 70.5 us
  Pallas kernels  65.5 us (93%)
  local copies, waits for them, and re-layouts  4.31 us (6%)
    pallas_call x1, Pallas kernels, local(): pl.pallas_call(kernel, out_shape=(jax.ShapeDtypeStruct((CHUNK, width), jn...  65.5 us
    unnamed x7, local copies, waits for them, and re-layouts  4.31 us

profile of v2, /device:TPU:1, one launch (start us, length us, event | category | flops | bytes accessed | tf_op | source)
XLA Modules:
  0.0 70.5 jit_solution(15553956446492386272)
XLA Ops:
  0.6 0.0 copy-start
  0.6 1.0 %copy-done = bf16[768,256]{1,0:T(8,128)(2,1)S(1)} copy-done((bf16[768,256]{1,0:T(8,128)(2,1)S(1)}, bf16[768,256]{1,0:T(8,128)(2,1)}, u32[]{:S(2)}) %copy-start) | copy-done | bytes 393240
  1.6 0.0 copy-start.1
  1.6 1.0 %copy-done.1 = bf16[768,256]{1,0:T(8,128)(2,1)S(1)} copy-done((bf16[768,256]{1,0:T(8,128)(2,1)S(1)}, bf16[768,256]{1,0:T(8,128)(2,1)}, u32[]{:S(2)}) %copy-start.1) | copy-done | bytes 393240
  2.6 65.5 %shard_map.49 = (f32[192,1024]{1,0:T(8,128)S(1)}, f32[192,1024]{1,0:T(8,128)S(1)}, f32[1,192]{1,0:T(1,128)S(1)}) custom-call(bf16[4,192,256]{2,1,0:T(8,128)(2,1)S(1)} %bitcast.4, bf16[4,192,256]{2,1,0:T(8,128)(2,1)S(1)} %bitcast.5), custom_call_target="tpu_custom_call" | custom-call | flops 3623878656 | bytes 1572864 | tf_op jit(solution)/shard_map/pallas_call | solution.py:261
  68.2 0.9 %copy.8 = f32[192,1024]{1,0:T(8,128)} copy(f32[192,1024]{1,0:T(8,128)S(1)} %get-tuple-element.12) | data formatting | bytes 1572864
  69.0 0.9 %copy.9 = f32[192,1024]{1,0:T(8,128)} copy(f32[192,1024]{1,0:T(8,128)S(1)} %get-tuple-element.13) | data formatting | bytes 1572864
  69.9 0.6 copy.10
Async XLA Ops:
  0.6 1.0 %copy-start = (bf16[768,256]{1,0:T(8,128)(2,1)S(1)}, bf16[768,256]{1,0:T(8,128)(2,1)}, u32[]{:S(2)}) copy-start(bf16[768,256]{1,0:T(8,128)(2,1)} %param.2) | copy-start | bytes 1179652
  1.6 1.0 %copy-start.1 = (bf16[768,256]{1,0:T(8,128)(2,1)S(1)}, bf16[768,256]{1,0:T(8,128)(2,1)}, u32[]{:S(2)}) copy-start(bf16[768,256]{1,0:T(8,128)(2,1)} %param.3) | copy-start | bytes 1179652

commit v3 on v2

--- a/solution.py
+++ b/solution.py
@@ -16,7 +16,7 @@
 CHUNK = 192
 COLS = 256
 X_AHEAD = 2
-GATES = (8, 7)
+GATES = (7, 7)
 LATE = 9
 SHIFT = 4
 ALONG = 16
@@ -132,8 +132,8 @@
 
         i = jnp.where(jnp.logical_not(late) & (n1 >= 4) & (n1 < 12) & (n1 % 2 == 0), 4 + (n1 - 4) // 2, -1)
         i = jnp.where(normal & (n2 >= 12) & (n2 < 16), n2 - 4, i)
-        i = jnp.where(second & (n >= LATE + 4) & (n < LATE + 8), n - LATE + 4, i)
-        i = jnp.where(late & (n >= LATE + 2) & (n < LATE + 10), n - LATE + 2, i)
+        i = jnp.where(second & (n >= LATE + 6) & (n < LATE + 10), n - LATE + 2, i)
+        i = jnp.where(late & (n >= LATE + 4) & (n < LATE + 12), n - LATE + 0, i)
 
         @pl.when(i >= 0)
         def _():
@@ -155,16 +155,16 @@
         def _():
             onward(t, 2, chunk_of(t, n1 - 4) + PARTS)
 
+    def sends_over_x(n, t):
+        across = flows[t][3]
         gate = GATES[t]
 
-        @pl.when(across & (n >= gate) & (n <= gate + 5))
+        @pl.when(across & (n >= gate) & (n <= gate))
         def _():
             @pl.when(n == gate)
             def _():
-                for k in range(3):
+                for k in range(2 * PARTS):
                     onward(t, 0, PARTS + k)
-
-            pl.when(n > gate)(lambda: onward(t, 0, n - gate + 2 + PARTS))
 
     def tile(t, slot):
         def rows_of(q):
@@ -193,17 +193,19 @@
         _, _, _, _, late, second = flows[t]
         n1, n2 = n - shifts(t)[0], n - shifts(t)[1]
         own_block = jnp.where(n < 8, jnp.clip(n - 3, 0, 3), PARTS)
-        farther = jnp.where(second, n - LATE + 4, n2 - 4)
+        farther = jnp.where(second, n - LATE + 2, n2 - 4)
         chunks = jnp.maximum(jnp.maximum(own_block, jnp.minimum(n1 - 4, 2 * PARTS)), farther)
-        chunks = jnp.where(late, jnp.maximum(own_block, n - LATE + 2), chunks)
+        chunks = jnp.where(late, jnp.maximum(own_block, n - LATE + 0), chunks)
         return jnp.minimum(chunks, SLOTS) // 2
 
-    apart = flows[0][4] | flows[1][4] | flows[0][5] | flows[1][5] | (z <= 1)
-    steps = jnp.where(apart, STEPS, STEPS - 4)
+    late, second = flows[0][4] | flows[1][4], flows[0][5] | flows[1][5]
+    steps = jnp.where(late, LATE + 13, jnp.where(second, LATE + 11, jnp.where(z <= 1, STEPS, STEPS - 4)))
 
     @pl.loop(0, steps)
     def _(n):
         pl.when((n < 2 * PARTS) & (n % 2 == 1))(lambda: over_x(n // 2))
+        for t in (1, 0):
+            sends_over_x(n, t)
         for t in range(2):
             arrivals(n, t)
         for t in range(2):

time: 70.7 us -> 69.3 us (0.980)
  Pallas kernels: 65.5 us -> 64.2 us
    pallas_call x1, Pallas kernels: 65.5 us -> 64.2 us  [local(): pl.pallas_call(kernel, out_shape=(jax.ShapeDtypeStruct((CHUNK, width), jn...]
where the time goes in v3:
time: 69.3 us; the launch traced here: 69.1 us
  Pallas kernels  64.2 us (93%)
  local copies, waits for them, and re-layouts  4.31 us (6%)
    pallas_call x1, Pallas kernels, local(): pl.pallas_call(kernel, out_shape=(jax.ShapeDtypeStruct((CHUNK, width), jn...  64.2 us
    unnamed x7, local copies, waits for them, and re-layouts  4.31 us

profile of v3, /device:TPU:1, one launch (start us, length us, event | category | flops | bytes accessed | tf_op | source)
XLA Modules:
  0.0 69.1 jit_solution(5191009692865795475)
XLA Ops:
  0.6 0.0 copy-start
  0.6 1.0 %copy-done = bf16[768,256]{1,0:T(8,128)(2,1)S(1)} copy-done((bf16[768,256]{1,0:T(8,128)(2,1)S(1)}, bf16[768,256]{1,0:T(8,128)(2,1)}, u32[]{:S(2)}) %copy-start) | copy-done | bytes 393240
  1.6 0.0 copy-start.1
  1.6 1.0 %copy-done.1 = bf16[768,256]{1,0:T(8,128)(2,1)S(1)} copy-done((bf16[768,256]{1,0:T(8,128)(2,1)S(1)}, bf16[768,256]{1,0:T(8,128)(2,1)}, u32[]{:S(2)}) %copy-start.1) | copy-done | bytes 393240
  2.6 64.2 %shard_map.49 = (f32[192,1024]{1,0:T(8,128)S(1)}, f32[192,1024]{1,0:T(8,128)S(1)}, f32[1,192]{1,0:T(1,128)S(1)}) custom-call(bf16[4,192,256]{2,1,0:T(8,128)(2,1)S(1)} %bitcast.4, bf16[4,192,256]{2,1,0:T(8,128)(2,1)S(1)} %bitcast.5), custom_call_target="tpu_custom_call" | custom-call | flops 3623878656 | bytes 1572864 | tf_op jit(solution)/shard_map/pallas_call | solution.py:263
  66.8 0.9 %copy.8 = f32[192,1024]{1,0:T(8,128)} copy(f32[192,1024]{1,0:T(8,128)S(1)} %get-tuple-element.12) | data formatting | bytes 1572864
  67.7 0.9 %copy.9 = f32[192,1024]{1,0:T(8,128)} copy(f32[192,1024]{1,0:T(8,128)S(1)} %get-tuple-element.13) | data formatting | bytes 1572864
  68.6 0.6 copy.10
Async XLA Ops:
  0.6 1.0 %copy-start = (bf16[768,256]{1,0:T(8,128)(2,1)S(1)}, bf16[768,256]{1,0:T(8,128)(2,1)}, u32[]{:S(2)}) copy-start(bf16[768,256]{1,0:T(8,128)(2,1)} %param.2) | copy-start | bytes 1179652
  1.6 1.0 %copy-start.1 = (bf16[768,256]{1,0:T(8,128)(2,1)S(1)}, bf16[768,256]{1,0:T(8,128)(2,1)}, u32[]{:S(2)}) copy-start(bf16[768,256]{1,0:T(8,128)(2,1)} %param.3) | copy-start | bytes 1179652
